TPU v7x, 128 devices: a whole 4x4x4 slice. The times are simulated.
128 devices in a mesh: tm: 8 (over y_lo, x), row: 4 (over z), col: 4 (over y_hi, core).
Axes of the slice: x: 4, y: 4 (y_hi: 2, y_lo: 2; y = y_hi * 2 + y_lo), z: 4, core: 2. Of those that a mesh axis runs over, the one named last changes fastest.
Arguments:
- tokens: bfloat16 [16, 64, 96, 384], P('tm', 'row', 'col'), may hold values from -8 to 8
- cache_first: bfloat16 [2, 64, 96, 384], P(None, 'row', 'col'), may hold values from -0.25 to 1.5
- cache_second: bfloat16 [2, 64, 96, 384], P(None, 'row', 'col'), may hold values from -0.25 to 1.5
- gain_first: float32 [384], replicated, may hold values from 0.1 to 1.9
- gain_second: float32 [384], replicated, may hold values from 0.1 to 1.9
- conv_first: bfloat16 [3, 3, 3, 384, 384], replicated, may hold values from -0.0625 to 0.0625
- conv_second: bfloat16 [3, 3, 3, 384, 384], replicated, may hold values from -0.0625 to 0.0625
- gain_attn: float32 [384], replicated, may hold values from 0.1 to 1.9
- query_weight: bfloat16 [384, 384], replicated, may hold values from -8 to 8
- key_weight: bfloat16 [384, 384], replicated, may hold values from -8 to 8
- value_weight: bfloat16 [384, 384], replicated, may hold values from -0.4375 to 0.4375
- out_weight: bfloat16 [384, 384], replicated, may hold values from -0.3125 to 0.3125
Outputs:
- decoded: bfloat16 [16, 64, 96, 384], P('tm', 'row', 'col')
All inputs are finite; a program needn't handle non-finite values.
Results may differ from a plain program's by a relative error of at most 0.019.
Values may be sent and summed in bfloat16 or wider, within the bound.
A program may use at most 128 MiB of HBM per device.

v0:
```python
import jax
import jax.numpy as jnp
from jax import lax
from jax.sharding import PartitionSpec as P


def passed_along(block, axis, distance):
    devices = range(lax.axis_size(axis))
    route = [(i - distance, i) for i in devices if i - distance in devices]
    return lax.ppermute(block, axis, route)


def padded_2(value, sides, width):
    for axis, dim in sides:
        count, length = (lax.axis_size(axis), value.shape[dim])
        up = [(i, (i + 1) % count) for i in range(count - 1)]
        down = [(j, i) for i, j in up]
        last = lax.slice_in_dim(value, length - width, length, axis=dim)
        initial = lax.slice_in_dim(value, 0, width, axis=dim)
        before = lax.ppermute(last, axis, up)
        after = lax.ppermute(initial, axis, down)
        value = jnp.concatenate([before, value, after], axis=dim)
    return value


def norm_gain(v, gain):
    return v * lax.rsqrt(jnp.mean(v * v, axis=-1, keepdims=True) + 1e-06) * gain


def causal_conv(frames, cache, kernel):
    count, rows, cols, chans = frames.shape
    before = passed_along(frames, "tm", 1)
    before = jnp.where(lax.axis_index("tm") == 0, cache, before)
    whole = jnp.concatenate([before, frames], axis=0)
    padded = padded_2(whole, (("row", 1), ("col", 2)), 1)
    windows = []
    for depth in range(3):
        for down in range(3):
            for across in range(3):
                windows.append(
                    padded[
                        depth : depth + count, down : down + rows, across : across + cols
                    ].reshape(-1, chans)
                )
    stacked = jnp.concatenate(windows, axis=1)
    result = jnp.dot(stacked, kernel.reshape(27 * chans, chans), preferred_element_type=jnp.float32)
    return result.reshape(count, rows, cols, chans)


def absorb(carry, query, keys, values, scale):
    running, total, accum = carry
    scores = jnp.einsum("fqc,fkc->fqk", query, keys, preferred_element_type=jnp.float32) * scale
    newtop = jnp.maximum(running, jnp.max(scores, axis=-1))
    expo = jnp.exp(scores - newtop[..., None])
    total = jnp.sum(expo, axis=-1)
    mixed = jnp.einsum(
        "fqk,fkc->fqc", expo.astype(jnp.bfloat16), values, preferred_element_type=jnp.float32
    )
    accum = mixed
    return (newtop, total, accum)


def on_device(
    tokens,
    cache_first,
    cache_second,
    gain_first,
    gain_second,
    conv_first,
    conv_second,
    gain_attn,
    query_weight,
    key_weight,
    value_weight,
    out_weight,
):
    count, rows, cols, chans = tokens.shape
    places = rows * cols
    scale = chans ** (-0.5)
    source = tokens.astype(jnp.float32)
    first_input = jax.nn.silu(norm_gain(source, gain_first)).astype(jnp.bfloat16)
    first_out = causal_conv(first_input, cache_first, conv_first)
    second_input = jax.nn.silu(norm_gain(first_out, gain_second)).astype(jnp.bfloat16)
    second_out = causal_conv(second_input, cache_second, conv_second)
    stream = (source + second_out).astype(jnp.bfloat16)
    normed = norm_gain(stream.astype(jnp.float32), gain_attn).astype(jnp.bfloat16)
    flat = normed.reshape(-1, chans)
    query = (
        jnp.dot(flat, query_weight, preferred_element_type=jnp.float32)
        .astype(jnp.bfloat16)
        .reshape(count, places, chans)
    )
    start_state = (
        jnp.full((count, places), -1e30, jnp.float32),
        jnp.zeros((count, places), jnp.float32),
        jnp.zeros((count, places, chans), jnp.float32),
    )
    keys = (
        jnp.dot(flat, key_weight, preferred_element_type=jnp.float32)
        .astype(jnp.bfloat16)
        .reshape(count, places, chans)
    )
    values = (
        jnp.dot(flat, value_weight, preferred_element_type=jnp.float32)
        .astype(jnp.bfloat16)
        .reshape(count, places, chans)
    )
    running, total, accum = absorb(
        start_state,
        query,
        lax.all_gather(keys, ("row", "col"), axis=1, tiled=True),
        lax.all_gather(values, ("row", "col"), axis=1, tiled=True),
        scale,
    )
    attended = (accum / total[..., None]).astype(jnp.bfloat16)
    projected = jnp.dot(attended.reshape(-1, chans), out_weight, preferred_element_type=jnp.float32)
    decoded = stream.astype(jnp.float32) + projected.reshape(count, rows, cols, chans)
    return decoded.astype(jnp.bfloat16)


def solution(mesh):
    placed = (
        P("tm", "row", "col", None),
        P(None, "row", "col", None),
        P(None, "row", "col", None),
        P(),
        P(),
        P(),
        P(),
        P(),
        P(),
        P(),
        P(),
        P(),
    )
    return jax.shard_map(
        on_device,
        mesh=mesh,
        in_specs=placed,
        out_specs=P("tm", "row", "col", None),
        check_vma=False,
    )
```

profile of v0, /device:TPU:1, one launch (start us, length us, event | category | flops | bytes accessed | tf_op | source)
XLA Modules:
  0.0 296.3 jit_solution(1504051326890316947)
XLA Ops:
  6.5 1.3 fusion.14
  7.9 1.5 fusion.21
  9.3 4.0 %collective-permute-start = (bf16[2,16,24,384]{3,2,1,0:T(8,128)(2,1)S(1)}, bf16[2,16,24,384]{3,2,1,0:T(8,128)(2,1)S(1)}, u32[]{:S(2)}, u32[]{:S(2)}) collective-permute-start(bf16[2,16,24,384]{3,2,1,0:T(8,128)(2,1)S(1)} %fusion.21), channel_id=1, source_target_pairs={{0,16},{16,32},{32,48},{48,64},{64,80},{80,96},{96,112},{1,17},{17... | collective-permute-start | bytes 1769480 | tf_op jit(solution)/shard_map/ppermute | solution.py:10
  13.3 11.9 %collective-permute-done = bf16[2,16,24,384]{3,2,1,0:T(8,128)(2,1)S(1)} collective-permute-done((bf16[2,16,24,384]{3,2,1,0:T(8,128)(2,1)S(1)}, bf16[2,16,24,384]{3,2,1,0:T(8,128)(2,1)S(1)}, u32[]{:S(2)}, u32[]{:S(2)}) %collective-permute-start) | collective-permute-done | bytes 589856 | tf_op jit(solution)/shard_map/ppermute | solution.py:10
  25.3 1.1 broadcast_select_fusion.1
  26.4 3.5 %collective-permute-start.1 = (bf16[4,1,24,384]{3,2,1,0:T(8,128)(2,1)S(1)}, bf16[4,1,24,384]{3,2,1,0:T(8,128)(2,1)S(1)}, u32[]{:S(2)}, u32[]{:S(2)}) collective-permute-start(bf16[4,1,24,384]{3,2,1,0:T(8,128)(2,1)S(1)} %get-tuple-element.19), channel_id=1, source_target_pairs={{0,4},{4,8},{8,12},{1,5},{5,9},{9,13},{2,6},{6,10},{10,14},{3,7},{... | collective-permute-start | bytes 221192 | tf_op jit(solution)/shard_map/ppermute | solution.py:20
  30.0 1.3 collective-permute-start.2
  31.4 3.9 %collective-permute-done.2 = bf16[4,1,24,384]{3,2,1,0:T(8,128)(2,1)S(1)} collective-permute-done((bf16[4,1,24,384]{3,2,1,0:T(8,128)(2,1)S(1)}, bf16[4,1,24,384]{3,2,1,0:T(8,128)(2,1)S(1)}, u32[]{:S(2)}, u32[]{:S(2)}) %collective-permute-start.2) | collective-permute-done | bytes 73760 | tf_op jit(solution)/shard_map/ppermute | solution.py:21
  35.5 4.7 %collective-permute-start.4 = (bf16[4,18,1,384]{3,2,1,0:T(2,128)(2,1)S(1)}, bf16[4,18,1,384]{3,2,1,0:T(2,128)(2,1)S(1)}, u32[]{:S(2)}, u32[]{:S(2)}) collective-permute-start(bf16[4,18,1,384]{3,2,1,0:T(2,128)(2,1)S(1)} %get-tuple-element.11), channel_id=1, source_target_pairs={{1,0},{2,1},{3,2},{5,4},{6,5},{7,6},{9,8},{10,9},{11,10},{13,12},{... | collective-permute-start | bytes 165896 | tf_op jit(solution)/shard_map/ppermute | solution.py:21
  40.2 4.7 %collective-permute-start.3 = (bf16[4,18,1,384]{3,2,1,0:T(2,128)(2,1)S(1)}, bf16[4,18,1,384]{3,2,1,0:T(2,128)(2,1)S(1)}, u32[]{:S(2)}, u32[]{:S(2)}) collective-permute-start(bf16[4,18,1,384]{3,2,1,0:T(2,128)(2,1)S(1)} %get-tuple-element.12), channel_id=1, source_target_pairs={{0,1},{1,2},{2,3},{4,5},{5,6},{6,7},{8,9},{9,10},{10,11},{12,13},{... | collective-permute-start | bytes 165896 | tf_op jit(solution)/shard_map/ppermute | solution.py:20
  45.4 1.2 collective-permute-done.3
  46.6 2.3 pad_maximum_fusion
  54.0 0.8 slice-done.1
  54.8 9.0 %multiply_reduce_fusion.1 = (f32[2,16,24]{2,1,0:T(8,128)S(1)}, f32[2,16,24,384]{3,2,1,0:T(8,128)S(1)}) fusion(bf16[2,16,24,10368]{3,2,1,0:T(8,128)(2,1)S(1)} %slice_dynamic-update-slice_fusion.24, bf16[10368,384,1,1]{1,0,3,2:T(8,128)(2,1)S(1)} %bitcast.43), kind=kOutput, calls=%fused_computation.40 | convolution fusion | flops 6115884032 | bytes 25070592 | tf_op jit(solution)/shard_map/dot_general | solution.py:46
  64.2 3.1 %collective-permute-start.5 = (bf16[2,16,24,384]{3,2,1,0:T(8,128)(2,1)S(1)}, bf16[2,16,24,384]{3,2,1,0:T(8,128)(2,1)S(1)}, u32[]{:S(2)}, u32[]{:S(2)}) collective-permute-start(bf16[2,16,24,384]{3,2,1,0:T(8,128)(2,1)S(1)} %multiply_convert_fusion), channel_id=1, source_target_pairs={{0,16},{16,32},{32,48},{48,64},{64,80},{80,96},{96,112},{1,17},{17... | collective-permute-start | bytes 1769480 | tf_op jit(solution)/shard_map/ppermute | solution.py:10
  67.3 10.5 %collective-permute-done.5 = bf16[2,16,24,384]{3,2,1,0:T(8,128)(2,1)S(1)} collective-permute-done((bf16[2,16,24,384]{3,2,1,0:T(8,128)(2,1)S(1)}, bf16[2,16,24,384]{3,2,1,0:T(8,128)(2,1)S(1)}, u32[]{:S(2)}, u32[]{:S(2)}) %collective-permute-start.5) | collective-permute-done | bytes 589856 | tf_op jit(solution)/shard_map/ppermute | solution.py:10
  77.9 3.5 %collective-permute-start.6 = (bf16[4,1,24,384]{3,2,1,0:T(8,128)(2,1)S(1)}, bf16[4,1,24,384]{3,2,1,0:T(8,128)(2,1)S(1)}, u32[]{:S(2)}, u32[]{:S(2)}) collective-permute-start(bf16[4,1,24,384]{3,2,1,0:T(8,128)(2,1)S(1)} %get-tuple-element.15), channel_id=1, source_target_pairs={{0,4},{4,8},{8,12},{1,5},{5,9},{9,13},{2,6},{6,10},{10,14},{3,7},{... | collective-permute-start | bytes 221192 | tf_op jit(solution)/shard_map/ppermute | solution.py:20
  81.5 1.5 collective-permute-start.7
  83.0 3.6 %collective-permute-done.7 = bf16[4,1,24,384]{3,2,1,0:T(8,128)(2,1)S(1)} collective-permute-done((bf16[4,1,24,384]{3,2,1,0:T(8,128)(2,1)S(1)}, bf16[4,1,24,384]{3,2,1,0:T(8,128)(2,1)S(1)}, u32[]{:S(2)}, u32[]{:S(2)}) %collective-permute-start.7) | collective-permute-done | bytes 73760 | tf_op jit(solution)/shard_map/ppermute | solution.py:21
  86.7 1.9 collective-permute-start.9
  88.7 5.9 %collective-permute-start.8 = (bf16[4,18,1,384]{3,2,1,0:T(2,128)(2,1)S(1)}, bf16[4,18,1,384]{3,2,1,0:T(2,128)(2,1)S(1)}, u32[]{:S(2)}, u32[]{:S(2)}) collective-permute-start(bf16[4,18,1,384]{3,2,1,0:T(2,128)(2,1)S(1)} %get-tuple-element.8), channel_id=1, source_target_pairs={{0,1},{1,2},{2,3},{4,5},{5,6},{6,7},{8,9},{9,10},{10,11},{12,13},{... | collective-permute-start | bytes 165896 | tf_op jit(solution)/shard_map/ppermute | solution.py:20
  95.1 1.2 collective-permute-done.8
  96.3 2.1 pad_maximum_fusion.1
  103.2 12.1 %fusion.22 = (f32[2,16,24]{2,1,0:T(8,128)S(1)}, bf16[2,16,24,384]{3,2,1,0:T(8,128)(2,1)S(1)}) fusion(bf16[2,16,24,10368]{3,2,1,0:T(8,128)(2,1)S(1)} %slice_dynamic-update-slice_fusion, bf16[10368,384,1,1]{1,0,3,2:T(8,128)(2,1)} %bitcast.44, bf16[2,16,24,384]{3,2,1,0:T(8,128)(2,1)S(1)} %copy-done.1), kind=kOutput, calls=%fused_computation.36 | convolution fusion | flops 6117063680 | bytes 25070592 | tf_op jit(solution)/shard_map/dot_general | solution.py:46
  115.6 1.4 convolution_convert_fusion.1
  117.3 1.3 convolution_convert_fusion
  119.1 79.2 %all-gather.3.cloned.1.call-done = bf16[2,6144,384]{2,1,0:T(8,128)(2,1)} async-done(((bf16[2,384,384]{2,1,0:T(8,128)(2,1)}), bf16[2,6144,384]{2,1,0:T(8,128)(2,1)}) %all-gather.3.cloned.1.call-update) | async-done | bytes 9437200 | tf_op jit(solution)/shard_map/all_gather | solution.py:111
  198.4 16.0 %multiply_reduce_fusion = (f32[2,384]{1,0:T(2,128)S(1)}, f32[2,384,6144]{2,1,0:T(8,128)}) fusion(bf16[2,384,384]{2,1,0:T(8,128)(2,1)S(1)} %bitcast.39, bf16[2,6144,384]{2,1,0:T(8,128)(2,1)} %all-gather.3.cloned.1.call-done), kind=kOutput, calls=%fused_computation.1 | convolution fusion | flops 3633315072 | bytes 28904448 | tf_op jit(solution)/shard_map/fqc,fkc->fqk/dot_general | solution.py:52
  214.4 9.7 %fusion = f32[2,384]{1,0:T(2,128)S(1)} fusion(f32[2,384,6144]{2,1,0:T(8,128)} %get-tuple-element.26, f32[2,384]{1,0:T(2,128)S(1)} %broadcast_maximum_fusion), kind=kLoop, calls=%fused_computation.2 | loop fusion | flops 14155008 | bytes 18880512 | tf_op jit(solution)/shard_map/reduce_sum | solution.py:55
  224.0 52.1 %all-gather.5.cloned.1.call-done = bf16[2,6144,384]{2,1,0:T(8,128)(2,1)} async-done(((bf16[2,384,384]{2,1,0:T(8,128)(2,1)}), bf16[2,6144,384]{2,1,0:T(8,128)(2,1)}) %all-gather.5.cloned.1.call-update) | async-done | bytes 9437200 | tf_op jit(solution)/shard_map/all_gather | solution.py:112
  276.1 11.9 %fusion.10 = bf16[2,384,384]{2,1,0:T(8,128)(2,1)S(1)} fusion(bf16[2,6144,384]{2,1,0:T(8,128)(2,1)} %all-gather.5.cloned.1.call-done, f32[2,384,6144]{2,1,0:T(8,128)} %get-tuple-element.26, f32[2,384]{1,0:T(2,128)S(1)} %broadcast_maximum_fusion, f32[2,384]{1,0:T(2,128)S(1)} %fusion), kind=kOutput, calls=%fused_computation.22 | convolution fusion | flops 3638624256 | bytes 28907520 | tf_op jit(solution)/shard_map/fqk,fkc->fqc/dot_general | solution.py:56
  288.1 1.4 fusion.9
  (98 shorter events, 12.5 us)
Async XLA Ops:
  6.5 109.0 %copy-start = (bf16[384,384]{1,0:T(8,128)(2,1)S(1)}, bf16[384,384]{1,0:T(8,128)(2,1)}, u32[]{:S(2)}) copy-start(bf16[384,384]{1,0:T(8,128)(2,1)} %param.21) | copy-start | bytes 884740
  6.5 191.8 %all-gather.3.cloned.1.call-start = ((), (), s32[]{:S(2)}) async-start(), calls=%async_computation | async-start | bytes 10027008 | tf_op jit(solution)/shard_map/all_gather | solution.py:111
  9.3 15.9 %collective-permute-start = (bf16[2,16,24,384]{3,2,1,0:T(8,128)(2,1)S(1)}, bf16[2,16,24,384]{3,2,1,0:T(8,128)(2,1)S(1)}, u32[]{:S(2)}, u32[]{:S(2)}) collective-permute-start(bf16[2,16,24,384]{3,2,1,0:T(8,128)(2,1)S(1)} %fusion.21), channel_id=1, source_target_pairs={{0,16},{16,32},{32,48},{48,64},{64,80},{80,96},{96,112},{1,17},{17... | collective-permute-start | bytes 1769480 | tf_op jit(solution)/shard_map/ppermute | solution.py:10
  26.4 4.9 %collective-permute-start.1 = (bf16[4,1,24,384]{3,2,1,0:T(8,128)(2,1)S(1)}, bf16[4,1,24,384]{3,2,1,0:T(8,128)(2,1)S(1)}, u32[]{:S(2)}, u32[]{:S(2)}) collective-permute-start(bf16[4,1,24,384]{3,2,1,0:T(8,128)(2,1)S(1)} %get-tuple-element.19), channel_id=1, source_target_pairs={{0,4},{4,8},{8,12},{1,5},{5,9},{9,13},{2,6},{6,10},{10,14},{3,7},{... | collective-permute-start | bytes 221192 | tf_op jit(solution)/shard_map/ppermute | solution.py:20
  30.0 5.3 %collective-permute-start.2 = (bf16[4,1,24,384]{3,2,1,0:T(8,128)(2,1)S(1)}, bf16[4,1,24,384]{3,2,1,0:T(8,128)(2,1)S(1)}, u32[]{:S(2)}, u32[]{:S(2)}) collective-permute-start(bf16[4,1,24,384]{3,2,1,0:T(8,128)(2,1)S(1)} %get-tuple-element.20), channel_id=1, source_target_pairs={{4,0},{8,4},{12,8},{5,1},{9,5},{13,9},{6,2},{10,6},{14,10},{7,3},{... | collective-permute-start | bytes 221192 | tf_op jit(solution)/shard_map/ppermute | solution.py:21
  35.5 9.9 %collective-permute-start.4 = (bf16[4,18,1,384]{3,2,1,0:T(2,128)(2,1)S(1)}, bf16[4,18,1,384]{3,2,1,0:T(2,128)(2,1)S(1)}, u32[]{:S(2)}, u32[]{:S(2)}) collective-permute-start(bf16[4,18,1,384]{3,2,1,0:T(2,128)(2,1)S(1)} %get-tuple-element.11), channel_id=1, source_target_pairs={{1,0},{2,1},{3,2},{5,4},{6,5},{7,6},{9,8},{10,9},{11,10},{13,12},{... | collective-permute-start | bytes 165896 | tf_op jit(solution)/shard_map/ppermute | solution.py:21
  40.2 6.5 %collective-permute-start.3 = (bf16[4,18,1,384]{3,2,1,0:T(2,128)(2,1)S(1)}, bf16[4,18,1,384]{3,2,1,0:T(2,128)(2,1)S(1)}, u32[]{:S(2)}, u32[]{:S(2)}) collective-permute-start(bf16[4,18,1,384]{3,2,1,0:T(2,128)(2,1)S(1)} %get-tuple-element.12), channel_id=1, source_target_pairs={{0,1},{1,2},{2,3},{4,5},{5,6},{6,7},{8,9},{9,10},{10,11},{12,13},{... | collective-permute-start | bytes 165896 | tf_op jit(solution)/shard_map/ppermute | solution.py:20
  51.1 2.9 slice-start
  51.5 1.3 copy-start.1
  51.5 1.3 copy-start.6
  52.1 2.7 slice-start.1
  54.8 9.0 %copy-start.7 = (f32[384]{0:T(512)S(1)}, f32[384]{0:T(512)}, u32[]{:S(2)}) copy-start(f32[384]{0:T(512)} %param.16) | copy-start | bytes 4612
  54.8 23.0 %copy-start.2 = (bf16[2,16,24,384]{3,2,1,0:T(8,128)(2,1)S(1)}, bf16[2,16,24,384]{3,2,1,0:T(8,128)(2,1)}, u32[]{:S(2)}) copy-start(bf16[2,16,24,384]{3,2,1,0:T(8,128)(2,1)} %param.14) | copy-start | bytes 1769476
  64.2 13.5 %collective-permute-start.5 = (bf16[2,16,24,384]{3,2,1,0:T(8,128)(2,1)S(1)}, bf16[2,16,24,384]{3,2,1,0:T(8,128)(2,1)S(1)}, u32[]{:S(2)}, u32[]{:S(2)}) collective-permute-start(bf16[2,16,24,384]{3,2,1,0:T(8,128)(2,1)S(1)} %multiply_convert_fusion), channel_id=1, source_target_pairs={{0,16},{16,32},{32,48},{48,64},{64,80},{80,96},{96,112},{1,17},{17... | collective-permute-start | bytes 1769480 | tf_op jit(solution)/shard_map/ppermute | solution.py:10
  77.9 5.1 %collective-permute-start.6 = (bf16[4,1,24,384]{3,2,1,0:T(8,128)(2,1)S(1)}, bf16[4,1,24,384]{3,2,1,0:T(8,128)(2,1)S(1)}, u32[]{:S(2)}, u32[]{:S(2)}) collective-permute-start(bf16[4,1,24,384]{3,2,1,0:T(8,128)(2,1)S(1)} %get-tuple-element.15), channel_id=1, source_target_pairs={{0,4},{4,8},{8,12},{1,5},{5,9},{9,13},{2,6},{6,10},{10,14},{3,7},{... | collective-permute-start | bytes 221192 | tf_op jit(solution)/shard_map/ppermute | solution.py:20
  81.5 5.1 %collective-permute-start.7 = (bf16[4,1,24,384]{3,2,1,0:T(8,128)(2,1)S(1)}, bf16[4,1,24,384]{3,2,1,0:T(8,128)(2,1)S(1)}, u32[]{:S(2)}, u32[]{:S(2)}) collective-permute-start(bf16[4,1,24,384]{3,2,1,0:T(8,128)(2,1)S(1)} %get-tuple-element.16), channel_id=1, source_target_pairs={{4,0},{8,4},{12,8},{5,1},{9,5},{13,9},{6,2},{10,6},{14,10},{7,3},{... | collective-permute-start | bytes 221192 | tf_op jit(solution)/shard_map/ppermute | solution.py:21
  86.7 8.3 %collective-permute-start.9 = (bf16[4,18,1,384]{3,2,1,0:T(2,128)(2,1)S(1)}, bf16[4,18,1,384]{3,2,1,0:T(2,128)(2,1)S(1)}, u32[]{:S(2)}, u32[]{:S(2)}) collective-permute-start(bf16[4,18,1,384]{3,2,1,0:T(2,128)(2,1)S(1)} %get-tuple-element.7), channel_id=1, source_target_pairs={{1,0},{2,1},{3,2},{5,4},{6,5},{7,6},{9,8},{10,9},{11,10},{13,12},{... | collective-permute-start | bytes 165896 | tf_op jit(solution)/shard_map/ppermute | solution.py:21
  88.7 7.7 %collective-permute-start.8 = (bf16[4,18,1,384]{3,2,1,0:T(2,128)(2,1)S(1)}, bf16[4,18,1,384]{3,2,1,0:T(2,128)(2,1)S(1)}, u32[]{:S(2)}, u32[]{:S(2)}) collective-permute-start(bf16[4,18,1,384]{3,2,1,0:T(2,128)(2,1)S(1)} %get-tuple-element.8), channel_id=1, source_target_pairs={{0,1},{1,2},{2,3},{4,5},{5,6},{6,7},{8,9},{9,10},{10,11},{12,13},{... | collective-permute-start | bytes 165896 | tf_op jit(solution)/shard_map/ppermute | solution.py:20
  103.2 12.1 %copy-start.8 = (f32[384]{0:T(512)S(1)}, f32[384]{0:T(512)}, u32[]{:S(2)}) copy-start(f32[384]{0:T(512)} %param.19) | copy-start | bytes 4612
  103.2 14.1 %copy-start.3 = (bf16[384,384]{1,0:T(8,128)(2,1)S(1)}, bf16[384,384]{1,0:T(8,128)(2,1)}, u32[]{:S(2)}) copy-start(bf16[384,384]{1,0:T(8,128)(2,1)} %param.22) | copy-start | bytes 884740
  115.3 3.3 %copy-start.4 = (bf16[384,384]{1,0:T(8,128)(2,1)S(1)}, bf16[384,384]{1,0:T(8,128)(2,1)}, u32[]{:S(2)}) copy-start(bf16[384,384]{1,0:T(8,128)(2,1)} %param.20) | copy-start | bytes 884740
  116.9 159.2 %all-gather.5.cloned.1.call-start = ((), (), s32[]{:S(2)}) async-start(), calls=%async_computation.1 | async-start | bytes 10027008 | tf_op jit(solution)/shard_map/all_gather | solution.py:112
  224.0 64.0 %copy-start.5 = (bf16[384,384]{1,0:T(8,128)(2,1)S(1)}, bf16[384,384]{1,0:T(8,128)(2,1)}, u32[]{:S(2)}) copy-start(bf16[384,384]{1,0:T(8,128)(2,1)} %param.23) | copy-start | bytes 884740
Sparse Core Ops, SparseCore 0:
  117.1 81.2 all-gather.2
  200.9 75.2 all-gather.4
where the time goes:
time: 297 us; the launch traced here: 296 us
  waiting for transfers between devices  164 us (55%)
  matrix products  53.5 us (18%)
  starting transfers between devices  34.5 us (12%)
  other arithmetic  21.1 us (7%)
  between operations  14.1 us (5%)
  local copies, waits for them, and re-layouts  9.11 us (3%)
    all_gather x1, waiting for transfers between devices, on_device(): lax.all_gather(keys, ('row', 'col'), axis=1, tiled=True)  79.2 us
    all_gather x1, waiting for transfers between devices, on_device(): lax.all_gather(values, ('row', 'col'), axis=1, tiled=True)  52.1 us
    ppermute x2, waiting for transfers between devices, passed_along(): return lax.ppermute(block, axis, route)  22.4 us
    dot_general x2, matrix products, causal_conv(): jnp.dot(stacked, kernel.reshape(27 * chans, chans), preferred_element_typ...  21.1 us
    ppermute x4, starting transfers between devices, padded_2(): before = lax.ppermute(last, axis, up)  17.7 us
    dot_general x1, matrix products, absorb(): jnp.einsum('fqc,fkc->fqk', query, keys, preferred_element_type=jnp.float32)  16 us
    dot_general x1, matrix products, absorb(): jnp.einsum('fqk,fkc->fqc', expo.astype(jnp.bfloat16), values, preferred_e...  11.9 us
    reduce_sum x1, other arithmetic, absorb(): total = jnp.sum(expo, axis=-1)  9.67 us
  transfers between devices with their start and end apart: 12, of which 9 were waited for; matrix products, arithmetic and copies ran while one was open for 10% of the time, Pallas kernels for 0%

commit v1 on v0

v1 whole, which is shorter than its diff:
```python
import functools
import math

import jax
import jax.numpy as jnp
from jax import lax
from jax.experimental import pallas as pl
from jax.experimental.pallas import tpu as pltpu
from jax.sharding import PartitionSpec as P

MESH = pl.DeviceIdType.MESH
F32 = jnp.float32
BF16 = jnp.bfloat16
C = 384
SIDES = [(dr, dc) for dr in (-1, 0, 1) for dc in (-1, 0, 1) if (dr, dc) != (0, 0)]
TILE = 8


def normed_by(v, gain):
    return v * lax.rsqrt(jnp.mean(v * v, axis=-1, keepdims=True) + 1e-06) * gain


def silu(v):
    return v / (1.0 + jnp.exp(-v))


def conv_kernel(
    tok, cache1, cache2, gain1, gain2, gain_a, w1, w2,
    stream_out, normed_out,
    wbuf, views, lift, held, acc, edges, cache_edges, halo_c, halo_r, halo_k, halo_t,
    w_sem, send_sem, recv_sem,
):
    ntm, nrow, ncol = (lax.axis_size(a) for a in ("tm", "row", "col"))
    tm, row, col = (lax.axis_index(a) for a in ("tm", "row", "col"))
    cols, rows = tok.shape[1], tok.shape[2]
    flat = cols * rows

    weights = []
    for stage, src in ((0, w1), (1, w2)):
        for a in (2, 1, 0):
            for c in range(3):
                copy = pltpu.make_async_copy(
                    src.at[a, :, c], wbuf.at[stage, a, c], w_sem.at[stage, a]
                )
                copy.start()
                weights.append((stage, a, copy))

    def wait_weights(stage, a):
        for s, b, copy in weights:
            if (s, b) == (stage, a):
                copy.wait()

    def there(dr, dc):
        ok = (row + dr >= 0) & (row + dr < nrow)
        return ok & (col + dc >= 0) & (col + dc < ncol)

    barrier = pltpu.get_barrier_semaphore()
    for dr, dc in SIDES:
        @pl.when(there(dr, dc))
        def _():
            pl.semaphore_signal(barrier, inc=1, device_id=(tm, row + dr, col + dc), device_id_type=MESH)

        @pl.when(there(dr, dc) & (tm > 0))
        def _():
            pl.semaphore_signal(barrier, inc=1, device_id=(tm - 1, row + dr, col + dc), device_id_type=MESH)

    @pl.when(tm > 0)
    def _():
        pl.semaphore_signal(barrier, inc=1, device_id=(tm - 1, row, col), device_id_type=MESH)

    def as_int(flag):
        return jnp.where(flag, 1, 0)

    around = (1 + as_int(row > 0) + as_int(row < nrow - 1)) * (1 + as_int(col > 0) + as_int(col < ncol - 1))
    expected = around - 1 + jnp.where(tm < ntm - 1, around, 0)

    def side_parts(ref_tile, ref_edge, dr, dc):
        if dr == 0:
            return ref_tile.at[:, cols - 1 if dc == 1 else 0]
        line = 1 if dr == 1 else 0
        if dc == 0:
            return ref_edge.at[:, line]
        return ref_edge.at[:, line, pl.ds(16 if dc == 1 else 0, 16)]

    def landing(stage, pair, dr, dc):
        if dr == 0:
            return halo_c.at[stage, pair, :, 0 if dc == 1 else 1]
        top = 0 if dr == 1 else 1
        if dc == 0:
            return halo_r.at[stage, pair, :, top]
        return halo_k.at[stage, pair, :, top, 0 if dc == 1 else 1]

    def side_copy(stage, group, k, ref_tile, ref_edge, target):
        dr, dc = SIDES[k]
        pair = 1 if group == 0 else 0
        return pltpu.make_async_remote_copy(
            src_ref=side_parts(ref_tile, ref_edge, dr, dc),
            dst_ref=landing(stage, pair, dr, dc),
            send_sem=send_sem.at[stage, group, k],
            recv_sem=recv_sem.at[stage, pair, k],
            device_id=(target, row + dr, col + dc),
            device_id_type=MESH,
        )

    def tile_copy(stage):
        return pltpu.make_async_remote_copy(
            src_ref=held.at[stage],
            dst_ref=halo_t.at[stage],
            send_sem=send_sem.at[stage, 1, TILE],
            recv_sem=recv_sem.at[stage, 0, TILE],
            device_id=(tm + 1, row, col),
            device_id_type=MESH,
        )

    def all_sends(stage, act):
        cache = (cache1, cache2)[stage]

        @pl.when(tm < ntm - 1)
        def _():
            act(tile_copy(stage))

        for k, (dr, dc) in enumerate(SIDES):
            @pl.when(there(dr, dc))
            def _():
                act(side_copy(stage, 0, k, held.at[stage], edges.at[stage], tm))

            @pl.when(there(dr, dc) & (tm < ntm - 1))
            def _():
                act(side_copy(stage, 1, k, held.at[stage], edges.at[stage], tm + 1))

    def cache_sends(stage, act):
        cache = (cache1, cache2)[stage]
        for k, (dr, dc) in enumerate(SIDES):
            @pl.when(there(dr, dc) & (tm == 0))
            def _():
                act(side_copy(stage, 2, k, cache, cache_edges.at[stage], 0))

    def wait_sides(stage, pair):
        for k, (dr, dc) in enumerate(SIDES):
            @pl.when(there(-dr, -dc))
            def _():
                side_copy(stage, 1 - pair, k, held.at[stage], edges.at[stage], tm).wait_recv()

    def take_edges(src, dst):
        for i in range(2):
            for line, at in ((0, 0), (1, rows - 1)):
                dst[i, line, 0:cols, :] = lift[1:cols + 1, 8 + at, :].astype(BF16)

    def lift_tile(src):
        def step(j, _):
            lift[j + 1, 8:8 + rows, :] = src[j].astype(F32)
            return 0
        lax.fori_loop(0, cols, step, 0)

    def edges_of(src, dst, i):
        lift_tile(src)
        dst[i, 0, 0:cols, :] = lift[1:cols + 1, 8, :].astype(BF16)
        dst[i, 1, 0:cols, :] = lift[1:cols + 1, 8 + rows - 1, :].astype(BF16)

    def build(stage, pair, i, src):
        slot = 2 * pair + i
        lift_tile(src)
        lift[0, 8:8 + rows, :] = halo_c[stage, pair, i, 0].astype(F32)
        lift[cols + 1, 8:8 + rows, :] = halo_c[stage, pair, i, 1].astype(F32)
        for top, at in ((0, 7), (1, 8 + rows)):
            lift[1:cols + 1, at, :] = halo_r[stage, pair, i, top, 0:cols, :].astype(F32)
            lift[0, at, :] = halo_k[stage, pair, i, top, 0].astype(F32)[cols - 17]
            lift[cols + 1, at, :] = halo_k[stage, pair, i, top, 1].astype(F32)[0]

        def step(j, _):
            for b in range(3):
                views[slot, j, :, b * C:(b + 1) * C] = lift[j, 7 + b:7 + b + rows, :].astype(BF16)
            return 0
        lax.fori_loop(0, cols + 2, step, 0)

    def taps(stage, frame, first, last):
        parts = [
            views[frame + a, c:c + cols].reshape(flat, 3 * C)
            for a in range(first, last) for c in range(3)
        ]
        left = jnp.concatenate(parts, axis=1) if len(parts) > 1 else parts[0]
        right = wbuf[stage, first:last].reshape((last - first) * 9 * C, C)
        return jnp.dot(left, right, preferred_element_type=F32)

    def conv(stage):
        wait_sides(stage, 1)
        for i in range(2):
            build(stage, 1, i, held.at[stage, i])
        wait_weights(stage, 2)
        wait_weights(stage, 1)
        acc[0] = taps(stage, 0, 2, 3)
        acc[1] = taps(stage, 1, 1, 3)

        @pl.when(tm > 0)
        def _():
            tile_copy(stage).wait_recv()

        wait_sides(stage, 0)
        for i in range(2):
            build(stage, 0, i, halo_t.at[stage, i])
        wait_weights(stage, 0)
        acc[0] += taps(stage, 0, 0, 2)
        acc[1] += taps(stage, 1, 0, 1)

    for k, (dr, dc) in enumerate(SIDES):
        @pl.when(jnp.logical_not(there(-dr, -dc)))
        def _():
            for stage in range(2):
                for pair in range(2):
                    ref = landing(stage, pair, dr, dc)
                    ref[...] = jnp.zeros(ref.shape, BF16)
    for ref in (edges, cache_edges):
        for stage in range(2):
            for i in range(2):
                for line in range(2):
                    ref[stage, i, line, 16:32, :] = jnp.zeros((16, C), BF16)

    @pl.when(tm == 0)
    def _():
        for stage, cache in ((0, cache1), (1, cache2)):
            for i in range(2):
                halo_t[stage, i] = cache[i]
                edges_of(cache.at[i], cache_edges.at[stage], i)

    def first(j, _):
        for i in range(2):
            v = tok[i, pl.ds(2 * j, 2)].astype(F32)
            held[0, i, pl.ds(2 * j, 2)] = silu(normed_by(v, gain1[...])).astype(BF16)
        return 0
    lax.fori_loop(0, cols // 2, first, 0)
    for i in range(2):
        edges_of(held.at[0, i], edges.at[0], i)

    pl.semaphore_wait(barrier, expected)
    all_sends(0, lambda copy: copy.start())
    for stage in range(2):
        cache_sends(stage, lambda copy: copy.start())
    conv(0)

    def second(j, _):
        for i in range(2):
            v = acc[i, pl.ds(j * 32, 32)]
            held[1, i, pl.ds(2 * j, 2)] = silu(normed_by(v, gain2[...])).astype(BF16).reshape(2, rows, C)
        return 0
    lax.fori_loop(0, cols // 2, second, 0)
    for i in range(2):
        edges_of(held.at[1, i], edges.at[1], i)
    all_sends(1, lambda copy: copy.start())
    conv(1)

    def last(j, _):
        for i in range(2):
            v = acc[i, pl.ds(j * 32, 32)] + tok[i, pl.ds(2 * j, 2)].astype(F32).reshape(32, C)
            v = v.astype(BF16)
            stream_out[i, pl.ds(j * 32, 32)] = v
            normed_out[i, pl.ds(j * 32, 32)] = normed_by(v.astype(F32), gain_a[...]).astype(BF16)
        return 0
    lax.fori_loop(0, cols // 2, last, 0)

    for stage in range(2):
        all_sends(stage, lambda copy: copy.wait_send())
        cache_sends(stage, lambda copy: copy.wait_send())


def convs(tok, cache1, cache2, gain1, gain2, gain_a, w1, w2):
    cols, rows = tok.shape[1], tok.shape[2]
    vmem = pl.BlockSpec(memory_space=pltpu.VMEM)
    hbm = pl.BlockSpec(memory_space=pl.ANY)
    out = jax.ShapeDtypeStruct((2, cols * rows, C), BF16)
    return pl.pallas_call(
        conv_kernel,
        out_shape=(out, out),
        in_specs=[vmem] * 6 + [hbm] * 2,
        out_specs=(vmem, vmem),
        scratch_shapes=[
            pltpu.VMEM((2, 3, 3, 3, C, C), BF16),
            pltpu.VMEM((4, cols + 2, rows, 3 * C), BF16),
            pltpu.VMEM((cols + 2, 32, C), F32),
            pltpu.VMEM((2, 2, cols, rows, C), BF16),
            pltpu.VMEM((2, cols * rows, C), F32),
            pltpu.VMEM((2, 2, 2, 32, C), BF16),
            pltpu.VMEM((2, 2, 2, 32, C), BF16),
            pltpu.VMEM((2, 2, 2, 2, rows, C), BF16),
            pltpu.VMEM((2, 2, 2, 2, 32, C), BF16),
            pltpu.VMEM((2, 2, 2, 2, 2, 16, C), BF16),
            pltpu.VMEM((2, 2, cols, rows, C), BF16),
            pltpu.SemaphoreType.DMA((2, 3)),
            pltpu.SemaphoreType.DMA((2, 3, 9)),
            pltpu.SemaphoreType.DMA((2, 2, 9)),
        ],
        compiler_params=pltpu.CompilerParams(
            collective_id=0, has_side_effects=True, vmem_limit_bytes=56 << 20
        ),
    )(tok, cache1, cache2, gain1, gain2, gain_a, w1, w2)


def attn_kernel(
    normed, stream, wq, wk, wv, wo,
    out,
    blocks, query, acc, top, total, mine, back,
    send_sem, recv_sem, back_sem,
):
    tm, row, col = (lax.axis_index(a) for a in ("tm", "row", "col"))
    nrow = lax.axis_size("row")
    places = normed.shape[1]
    frame = col // 2
    other = 1 - frame
    partner = (tm, row, lax.rem(col + 2, 4))
    sibling = (tm, row, col + 1 - 2 * lax.rem(col, 2))
    up = (tm, lax.rem(row + 1, nrow), col)
    down = (tm, lax.rem(row + nrow - 1, nrow), col)

    barrier = pltpu.get_barrier_semaphore()
    for device in (partner, sibling, up, down):
        pl.semaphore_signal(barrier, inc=1, device_id=device, device_id_type=MESH)
    pl.semaphore_wait(barrier, 4)

    sent = []

    def send(src, dst, device):
        rel, half, core = dst
        copy = pltpu.make_async_remote_copy(
            src_ref=src,
            dst_ref=blocks.at[rel, half, core],
            send_sem=send_sem.at[len(sent)],
            recv_sem=recv_sem.at[rel, half, core],
            device_id=device,
            device_id_type=MESH,
        )
        copy.start()
        sent.append(copy)

    def arrived(rel, half, core):
        pltpu.make_async_remote_copy(
            src_ref=blocks.at[rel, half, core],
            dst_ref=blocks.at[rel, half, core],
            send_sem=send_sem.at[0],
            recv_sem=recv_sem.at[rel, half, core],
            device_id=partner,
            device_id_type=MESH,
        ).wait_recv()

    send(normed.at[other], (0, 1, 0), partner)
    send(normed.at[frame], (3, 0, 0), up)
    send(normed.at[frame], (1, 0, 0), down)
    send(normed.at[frame], (0, 0, 1), sibling)
    blocks[0, 0, 0] = normed[frame]

    factor = math.log2(math.e) * C ** (-0.5)

    def ask(half):
        q = jnp.dot(blocks[0, half, 0], wq[...], preferred_element_type=F32).astype(BF16)
        q = lax.dot_general(q, wk[...], (((1,), (1,)), ((), ())), preferred_element_type=F32)
        query[half] = (q * factor).astype(BF16)

    ask(0)
    top[...] = jnp.full(top.shape, -1e30, F32)
    total[...] = jnp.zeros(total.shape, F32)
    acc[...] = jnp.zeros(acc.shape, F32)

    def absorb(rel, half):
        keys = blocks[rel, half].reshape(2 * places, C)

        def step(n, _):
            for h in range(2):
                at = pl.ds(n * 128, 128)
                s = lax.dot_general(query[h, at], keys, (((1,), (1,)), ((), ())), preferred_element_type=F32)
                before = top[h, at]
                now = jnp.maximum(before, jnp.max(s, axis=-1, keepdims=True))
                shrink = jnp.exp2(before - now)
                expo = jnp.exp2(s - now[:, 0:1])
                total[h, at] = total[h, at] * shrink + jnp.sum(expo, axis=-1, keepdims=True)
                mixed = jnp.dot(expo.astype(BF16), keys, preferred_element_type=F32)
                acc[h, at] = acc[h, at] * shrink[:, 0:1] + mixed
                top[h, at] = now
            return 0
        lax.fori_loop(0, places // 128, step, 0)

    arrived(0, 1, 0)
    send(blocks.at[0, 1, 0], (3, 1, 0), up)
    send(blocks.at[0, 1, 0], (1, 1, 0), down)
    send(blocks.at[0, 1, 0], (0, 1, 1), sibling)
    ask(1)
    arrived(3, 0, 0)
    send(blocks.at[3, 0, 0], (2, 0, 0), up)
    send(blocks.at[3, 0, 0], (3, 0, 1), sibling)
    arrived(1, 0, 0)
    send(blocks.at[1, 0, 0], (1, 0, 1), sibling)
    arrived(0, 0, 1)
    absorb(0, 0)
    arrived(0, 1, 1)
    absorb(0, 1)
    arrived(3, 1, 0)
    send(blocks.at[3, 1, 0], (3, 1, 1), sibling)
    arrived(1, 1, 0)
    send(blocks.at[1, 1, 0], (2, 1, 0), down)
    send(blocks.at[1, 1, 0], (1, 1, 1), sibling)
    arrived(3, 0, 1)
    absorb(3, 0)
    arrived(1, 0, 1)
    absorb(1, 0)
    arrived(2, 0, 0)
    send(blocks.at[2, 0, 0], (2, 0, 1), sibling)
    arrived(3, 1, 1)
    absorb(3, 1)
    arrived(2, 1, 0)
    send(blocks.at[2, 1, 0], (2, 1, 1), sibling)
    arrived(1, 1, 1)
    absorb(1, 1)
    arrived(2, 0, 1)
    absorb(2, 0)
    arrived(2, 1, 1)
    absorb(2, 1)

    def attended(h):
        mixed = (acc[h] / total[h][:, 0:1]).astype(BF16)
        return jnp.dot(mixed, wv[...], preferred_element_type=F32).astype(BF16)

    def finish(at, values):
        out[at] = (stream[at].astype(F32) + jnp.dot(values, wo[...], preferred_element_type=F32)).astype(BF16)

    mine[...] = attended(1)
    copy = pltpu.make_async_remote_copy(
        src_ref=mine, dst_ref=back, send_sem=back_sem.at[0], recv_sem=back_sem.at[1],
        device_id=partner, device_id_type=MESH,
    )
    copy.start()
    finish(frame, attended(0))
    copy.wait()
    finish(other, back[...])
    for copy in sent:
        copy.wait_send()


def attention(normed, stream, wq, wk, wv, wo):
    places = normed.shape[1]
    vmem = pl.BlockSpec(memory_space=pltpu.VMEM)
    return pl.pallas_call(
        attn_kernel,
        out_shape=jax.ShapeDtypeStruct(normed.shape, BF16),
        in_specs=[vmem] * 6,
        out_specs=vmem,
        scratch_shapes=[
            pltpu.VMEM((4, 2, 2, places, C), BF16),
            pltpu.VMEM((2, places, C), BF16),
            pltpu.VMEM((2, places, C), F32),
            pltpu.VMEM((2, places, 128), F32),
            pltpu.VMEM((2, places, 128), F32),
            pltpu.VMEM((places, C), BF16),
            pltpu.VMEM((places, C), BF16),
            pltpu.SemaphoreType.DMA((20,)),
            pltpu.SemaphoreType.DMA((4, 2, 2)),
            pltpu.SemaphoreType.DMA((2,)),
        ],
        compiler_params=pltpu.CompilerParams(
            collective_id=1, has_side_effects=True, vmem_limit_bytes=48 << 20
        ),
    )(normed, stream, wq, wk, wv, wo)


def on_device(
    tokens, cache_first, cache_second, gain_first, gain_second, conv_first, conv_second,
    gain_attn, query_weight, key_weight, value_weight, out_weight,
):
    count, rows, cols, chans = tokens.shape
    swap = lambda v: jnp.swapaxes(v, 1, 2)
    stream, normed = convs(
        swap(tokens), swap(cache_first), swap(cache_second),
        gain_first[None], gain_second[None], gain_attn[None], conv_first, conv_second,
    )
    out = attention(normed, stream, query_weight, key_weight, value_weight, out_weight)
    return swap(out.reshape(count, cols, rows, chans))


def solution(mesh):
    spread, kept = P("tm", "row", "col", None), P(None, "row", "col", None)
    return jax.shard_map(
        on_device,
        mesh=mesh,
        in_specs=(spread, kept, kept) + (P(),) * 9,
        out_specs=spread,
        check_vma=False,
    )
```

time: 297 us -> 136 us (0.46)
  waiting for transfers between devices: 164 us -> 0 us
  Pallas kernels: 0 us -> 124 us
  matrix products: 53.5 us -> 0 us
  starting transfers between devices: 34.5 us -> 0 us
  other arithmetic: 21.1 us -> 0 us
  between operations: 14.1 us -> 0.07 us
    all_gather x2 -> x0, waiting for transfers between devices: 131 us -> none  [the longest x1 79.2 us: on_device(): lax.all_gather(keys, ('row', 'col'), axis=1, tiled=True)]
    pallas_call x0 -> x2, Pallas kernels: none -> 124 us  [the longest x1 67.3 us: convs(): pl.pallas_call(conv_kernel, out_shape=(out, out), in_specs=[vmem] * 6 + [...]
    dot_general x8 -> x0, matrix products: 53.5 us -> none  [the longest x2 21.1 us: causal_conv(): jnp.dot(stacked, kernel.reshape(27 * chans, chans), preferred_element_typ...]
    ppermute x10 -> x0, starting transfers between devices: 34.2 us -> none  [the longest x4 17.7 us: padded_2(): before = lax.ppermute(last, axis, up)]
    ppermute x10 -> x0, waiting for transfers between devices: 32.5 us -> none  [the longest x2 22.4 us: passed_along(): return lax.ppermute(block, axis, route)]
    reduce_sum x2 -> x0, other arithmetic: 11 us -> none  [the longest x1 9.67 us: absorb(): total = jnp.sum(expo, axis=-1)]
    concatenate x6 -> x0, other arithmetic: 5.64 us -> none  [padded_2(): value = jnp.concatenate([before, value, after], axis=dim)]
    unnamed x70 -> x13, local copies, waits for them, and re-layouts: 8.56 us -> 4.09 us
  transfers between devices with their start and end apart: 12 -> 0, of which waited for: 9 -> 0; matrix products, arithmetic and copies ran while one was open for 10% -> 0% of each run, Pallas kernels for 0% -> 0%
where the time goes in v1:
time: 136 us; the launch traced here: 135 us
  Pallas kernels  124 us (91%)
  local copies, waits for them, and re-layouts  11.2 us (8%)
    pallas_call x1, Pallas kernels, convs(): pl.pallas_call(conv_kernel, out_shape=(out, out), in_specs=[vmem] * 6 + [...  67.3 us
    pallas_call x1, Pallas kernels, attention(): pl.pallas_call(attn_kernel, out_shape=jax.ShapeDtypeStruct(normed.shape,...  56.6 us
    unnamed x13, local copies, waits for them, and re-layouts  4.09 us

profile of v1, /device:TPU:1, one launch (start us, length us, event | category | flops | bytes accessed | tf_op | source)
XLA Modules:
  0.0 135.2 jit_solution(16520730328944525868)
XLA Ops:
  0.0 1.3 broadcast_in_dim.9.gain1
  1.3 1.3 broadcast_in_dim.10.gain2
  2.5 1.2 broadcast_in_dim.11.gain_a
  3.8 2.0 %copy.22 = bf16[2,16,24,384]{3,1,2,0:T(8,128)(2,1)} copy(bf16[2,16,24,384]{3,2,1,0:T(8,128)(2,1)} %param.12) | data formatting | bytes 1179648 | tf_op args[0]
  5.7 2.4 %copy_bitcast_fusion.1 = (bf16[2,24,16,384]{3,2,1,0:T(8,128)(2,1)}, bf16[2,24,16,384]{3,2,1,0:T(8,128)(2,1)}) fusion(bf16[2,16,24,384]{3,2,1,0:T(8,128)(2,1)} %param.14, bf16[2,16,24,384]{3,2,1,0:T(8,128)(2,1)} %param.13), kind=kLoop, calls=%fused_computation.1 | loop fusion | bytes 2359296 | tf_op jit(solution)/shard_map/transpose | solution.py:466
  8.2 0.0 copy-start.2
  8.2 0.0 copy-start.3
  8.2 0.0 copy-start.4
  8.2 0.0 copy-start.5
  8.2 67.3 %shard_map.118 = (bf16[2,384,384]{2,1,0:T(8,128)(2,1)}, bf16[2,384,384]{2,1,0:T(8,128)(2,1)}) custom-call(bf16[2,24,16,384]{3,2,1,0:T(8,128)(2,1)} %bitcast.12, bf16[2,24,16,384]{3,2,1,0:T(8,128)(2,1)} %get-tuple-element.10.cache1, bf16[2,24,16,384]{3,2,1,0:T(8,128)(2,1)} %get-tuple-element.9.cache2, f32[1,384]{1,0:T(1,128)} %broadcast_in_dim.9.gain1, ...), custom_call_target="tpu_custom_call" | custom-call | tf_op jit(solution)/shard_map/pallas_call | solution.py:270
  75.5 0.0 copy-done.2
  75.5 0.0 copy-done.3
  75.5 0.0 copy-done.4
  75.5 0.0 copy-done.5
  75.5 0.0 copy-start
  75.5 1.1 copy-done
  76.6 0.0 copy-start.1
  76.6 1.1 copy-done.1
  77.6 56.6 %shard_map.119 = bf16[2,384,384]{2,1,0:T(8,128)(2,1)S(1)} custom-call(bf16[2,384,384]{2,1,0:T(8,128)(2,1)S(1)} %copy-done.1, bf16[2,384,384]{2,1,0:T(8,128)(2,1)S(1)} %copy-done, bf16[384,384]{1,0:T(8,128)(2,1)S(1)} %copy-done.2, bf16[384,384]{1,0:T(8,128)(2,1)S(1)} %copy-done.3, bf16[384,384]{1,0:T(8,128)(2,1)S(1)} %copy-done.4, bf16[384,384]{1,0:T(8,128)(2,1)S(1)} %copy-done.5), custom_call_target="tpu_custom_call" | custom-call | tf_op jit(solution)/shard_map/pallas_call | solution.py:438
  134.2 0.9 copy.21
Async XLA Ops:
  8.2 67.3 %copy-start.2 = (bf16[384,384]{1,0:T(8,128)(2,1)S(1)}, bf16[384,384]{1,0:T(8,128)(2,1)}, u32[]{:S(2)}) copy-start(bf16[384,384]{1,0:T(8,128)(2,1)} %wq.1) | copy-start | bytes 884740
  8.2 67.3 %copy-start.3 = (bf16[384,384]{1,0:T(8,128)(2,1)S(1)}, bf16[384,384]{1,0:T(8,128)(2,1)}, u32[]{:S(2)}) copy-start(bf16[384,384]{1,0:T(8,128)(2,1)} %wk.1) | copy-start | bytes 884740
  8.2 67.3 %copy-start.4 = (bf16[384,384]{1,0:T(8,128)(2,1)S(1)}, bf16[384,384]{1,0:T(8,128)(2,1)}, u32[]{:S(2)}) copy-start(bf16[384,384]{1,0:T(8,128)(2,1)} %wv.1) | copy-start | bytes 884740
  8.2 67.3 %copy-start.5 = (bf16[384,384]{1,0:T(8,128)(2,1)S(1)}, bf16[384,384]{1,0:T(8,128)(2,1)}, u32[]{:S(2)}) copy-start(bf16[384,384]{1,0:T(8,128)(2,1)} %wo.1) | copy-start | bytes 884740
  75.5 1.1 copy-start
  76.6 1.1 copy-start.1

commit v2 on v0

v2 whole, which is shorter than its diff:
```python
import math

import jax
import jax.numpy as jnp
from jax import lax
from jax.experimental import pallas as pl
from jax.experimental.pallas import tpu as pltpu
from jax.sharding import PartitionSpec as P

MESH = pl.DeviceIdType.MESH
F32 = jnp.float32
BF16 = jnp.bfloat16
C, ROWS, COLS = 384, 16, 24
PLACES = ROWS * COLS
SIDES = [(dr, dc) for dr in (-1, 0, 1) for dc in (-1, 0, 1) if (dr, dc) != (0, 0)]
INNER = {8: -1, 9: 1}
SENT = {0: (((0, 9), (15, 24)), ((9, 15),)), 1: (((0, 8), (16, 24)), ((8, 16),))}
DONE = {0: (((0, 8), (16, 24)), ((8, 16),)), 1: (((0, 7), (17, 24)), ((7, 17),))}
BUILT = {0: (((0, 10), (16, 26)), ((10, 16),)), 1: (((0, 9), (17, 26)), ((9, 17),))}
PIECES = ((0, 224), (224, 160))
LIFTED = 32
LANES = C // 128


def normed_by(v, gain):
    return v * lax.rsqrt(jnp.mean(v * v, axis=-1, keepdims=True) + 1e-06) * gain


def each(lo, hi, body, unroll):
    def step(n, _):
        body(n)
        return 0
    lax.fori_loop(lo, hi, step, 0, unroll=min(unroll, hi - lo))


def silu(v):
    return v / (1.0 + jnp.exp(-v))


def kernel(
    tok, cache1, cache2, gain1, gain2, gain_a, w1, w2, wq, wk, wv, wo,
    out,
    wbuf, views, lift, tok_t, held, acc, cache_in,
    edge_o, edge_i, corner, cache_o, cache_i, cache_k,
    halo_c, halo_o, halo_i, halo_k, halo_t,
    normed, stream, blocks, query, mixed, top, total, mine, back,
    w_sem, cache_sem, send_sem, recv_sem, attn_send, attn_recv, back_sem,
):
    ntm, nrow, ncol = (lax.axis_size(a) for a in ("tm", "row", "col"))
    tm, row, col = (lax.axis_index(a) for a in ("tm", "row", "col"))
    partner = (tm, row, lax.rem(col + 2, ncol))
    sibling = (tm, row, col + 1 - 2 * lax.rem(col, 2))
    up = (tm, lax.rem(row + 1, nrow), col)
    down = (tm, lax.rem(row + nrow - 1, nrow), col)
    lines = lift.reshape(LANES, (COLS + 2) * LIFTED, 128)

    def put_line(at, first, v):
        for k in range(LANES):
            lines[k, pl.ds(first * LIFTED + 8 + at, v.shape[0], stride=LIFTED), :] = v[:, k * 128:(k + 1) * 128]

    def get_line(at, first, count):
        return jnp.concatenate([
            lines[k, pl.ds(first * LIFTED + 8 + at, count, stride=LIFTED), :] for k in range(LANES)
        ], axis=1)

    def put_column(j, at, v):
        for k in range(LANES):
            lift[k, j, 8 + at:8 + at + v.shape[0], :] = v[:, k * 128:(k + 1) * 128]

    def get_column(j, at, count):
        return jnp.concatenate([lift[k, j, 8 + at:8 + at + count, :] for k in range(LANES)], axis=1)

    def there(dr, dc):
        ok = (row + dr >= 0) & (row + dr < nrow)
        return ok & (col + dc >= 0) & (col + dc < ncol)

    barrier = pltpu.get_barrier_semaphore()
    for dr, dc in SIDES:
        @pl.when(there(dr, dc))
        def _():
            pl.semaphore_signal(barrier, inc=1, device_id=(tm, row + dr, col + dc), device_id_type=MESH)

        @pl.when(there(dr, dc) & (tm > 0))
        def _():
            pl.semaphore_signal(barrier, inc=1, device_id=(tm - 1, row + dr, col + dc), device_id_type=MESH)

    @pl.when(tm > 0)
    def _():
        pl.semaphore_signal(barrier, inc=1, device_id=(tm - 1, row, col), device_id_type=MESH)

    for device in (partner, sibling, up, down):
        pl.semaphore_signal(barrier, inc=1, device_id=device, device_id_type=MESH)

    def as_int(flag):
        return jnp.where(flag, 1, 0)

    around = (1 + as_int(row > 0) + as_int(row < nrow - 1)) * (1 + as_int(col > 0) + as_int(col < ncol - 1))
    expected = around - 1 + jnp.where(tm < ntm - 1, around, 0) + 4

    caches = [
        pltpu.make_async_copy(src, cache_in.at[stage], cache_sem.at[stage])
        for stage, src in ((0, cache1), (1, cache2))
    ]

    @pl.when(tm == 0)
    def _():
        for copy in caches:
            copy.start()

    weights = []
    for stage, src in ((0, w1), (1, w2)):
        for a in (2, 1, 0):
            for c in range(3):
                copy = pltpu.make_async_copy(
                    src.at[a, :, c],
                    wbuf.at[stage, c, :, :, pl.ds((2 - a) * C, C)],
                    w_sem.at[stage, a],
                )
                copy.start()
                weights.append((stage, a, copy))

    def wait_weights(stage, a):
        for s, b, copy in weights:
            if (s, b) == (stage, a):
                copy.wait()

    def step_of(k):
        return (INNER[k], 0) if k in INNER else SIDES[k]

    def side_copy(stage, group, k):
        dr, dc = step_of(k)
        pair = 1 if group == 0 else 0
        tile = halo_t if group == 2 else held
        e_o, e_i, e_k = (cache_o, cache_i, cache_k) if group == 2 else (edge_o, edge_i, corner)
        line, top_at = (1, 0) if dr == 1 else (0, 1)
        lr = 0 if dc == 1 else 1
        if k in INNER:
            src, dst = e_i.at[stage, line], halo_i.at[stage, pair, top_at]
        elif dr == 0:
            src, dst = tile.at[stage, :, COLS - 1 if dc == 1 else 0], halo_c.at[stage, pair, :, lr]
        elif dc == 0:
            src, dst = e_o.at[stage, line], halo_o.at[stage, pair, top_at]
        else:
            src, dst = e_k.at[stage], halo_k.at[stage, pair, top_at, lr]
        return pltpu.make_async_remote_copy(
            src_ref=src,
            dst_ref=dst,
            send_sem=send_sem.at[stage, group, k],
            recv_sem=recv_sem.at[stage, pair, k],
            device_id=(tm + 1 if group == 1 else tm, row + dr, col + dc),
            device_id_type=MESH,
        )

    def tile_copies(stage, part):
        made = []
        for n, (lo, hi) in enumerate(SENT[stage][part]):
            k = 10 + 2 * part + n
            made.append(pltpu.make_async_remote_copy(
                src_ref=held.at[stage, :, pl.ds(lo, hi - lo)],
                dst_ref=halo_t.at[stage, :, pl.ds(lo, hi - lo)],
                send_sem=send_sem.at[stage, 1, k],
                recv_sem=recv_sem.at[stage, 0, k],
                device_id=(tm + 1, row, col),
                device_id_type=MESH,
            ))
        return made

    def sides_in(part):
        return tuple(INNER) if part else tuple(range(8))

    def side_sends(stage, group, part, act):
        for k in sides_in(part):
            ok = there(*step_of(k))
            if group == 1:
                ok = ok & (tm < ntm - 1)
            if group == 2:
                ok = ok & (tm == 0)

            @pl.when(ok)
            def _():
                act(side_copy(stage, group, k))

    def tile_sends(stage, part, act):
        @pl.when(tm < ntm - 1)
        def _():
            for copy in tile_copies(stage, part):
                act(copy)

    def start(copy):
        copy.start()

    def wait_sides(stage, pair, part):
        for k in sides_in(part):
            dr, dc = step_of(k)

            @pl.when(there(-dr, -dc))
            def _():
                side_copy(stage, 1 - pair, k).wait_recv()

    def wait_tile(stage, part):
        @pl.when(tm > 0)
        def _():
            for copy in tile_copies(stage, part):
                copy.wait_recv()

    def take_lines(stage, i, part, e_o, e_k):
        for line, at in ((0, 0), (1, ROWS - 1)):
            if part == 0:
                both = [get_line(at, 1, 8), get_line(at, 17, 8)]
                e_o[stage, line, i] = jnp.concatenate(both, axis=0).astype(BF16)
        if part == 0:
            fill = jnp.zeros((2, C), F32)
            rows = []
            for at in (0, ROWS - 1):
                rows += [get_column(1, at, 1), get_column(COLS, at, 1), fill]
            return jnp.concatenate(rows, axis=0)

    def inner_lines():
        return [get_line(at, 9, 8) for at in (0, ROWS - 1)]

    def lift_columns(src, lo, hi):
        def step(j):
            put_column(j + 1, 0, src[j].astype(F32))
        each(lo, hi, step, 4)

    def lift_lines(stage, pair, i, part):
        for t, at in ((0, -1), (1, ROWS)):
            if part == 0:
                v = halo_o[stage, pair, t, i].astype(F32)
                put_line(at, 1, v[0:8])
                put_line(at, 17, v[8:16])
                for lr, j in ((0, 0), (1, COLS + 1)):
                    n = i * 8 + (1 - t) * 4 + (1 - lr)
                    put_column(j, at, halo_k[stage, pair, t, lr].astype(F32)[n:n + 1])
            else:
                put_line(at, 9, halo_i[stage, pair, t].astype(F32)[8 * i:8 * i + 8])
        if part == 0:
            put_column(0, 0, halo_c[stage, pair, i, 0].astype(F32))
            put_column(COLS + 1, 0, halo_c[stage, pair, i, 1].astype(F32))

    def build(slot, spans):
        def step(j):
            for b in range(3):
                views[slot, j, :, b * C:(b + 1) * C] = get_column(j, b - 1, ROWS).astype(BF16)
        for lo, hi in spans:
            each(lo, hi, step, 4)

    def window(slot, spans):
        return jnp.concatenate([
            jnp.concatenate(
                [views[slot, lo + c:hi + c].reshape((hi - lo) * ROWS, 3 * C) for c in range(3)], axis=1
            )
            for lo, hi in spans
        ], axis=0)

    def times(left, stage, lo, hi):
        right = wbuf[stage, :, :, :, lo:hi].reshape(9 * C, hi - lo)
        return jnp.dot(left, right, preferred_element_type=F32)

    def conv_own(stage):
        wait_sides(stage, 1, 0)
        wait_sides(stage, 1, 1)
        for i in range(2):
            lift_columns(held.at[stage, i], 0, COLS)
            lift_lines(stage, 1, i, 0)
            lift_lines(stage, 1, i, 1)
            build(2 + i, ((0, COLS + 2),))
        wait_weights(stage, 2)
        wait_weights(stage, 1)
        whole = ((0, COLS),)
        acc[...] = times(window(2, whole), stage, 0, 2 * C)
        acc[:, C:] += times(window(3, whole), stage, 0, C)

    def conv_before(stage, part):
        if stage == 0 and part == 0:
            wait_sides(0, 0, 1)
        if stage == 1 and part == 1:
            wait_sides(1, 0, 1)
        if part == 0:
            wait_sides(stage, 0, 0)
        wait_tile(stage, part)
        for i in range(2):
            for lo, hi in SENT[stage][part]:
                lift_columns(halo_t.at[stage, i], lo, hi)
            if part == 0:
                lift_lines(stage, 0, i, 0)
            if part == 1 or stage == 0:
                lift_lines(stage, 0, i, 1)
            build(i, BUILT[stage][part])
        if part == 0:
            wait_weights(stage, 0)
        spans = DONE[stage][part]
        near = times(window(1, spans), stage, C, 3 * C)
        far = times(window(0, spans), stage, 2 * C, 3 * C)
        n = 0
        for lo, hi in spans:
            size = (hi - lo) * ROWS
            at = slice(lo * ROWS, hi * ROWS)
            acc[at, 0:C] += near[n:n + size, 0:C] + far[n:n + size]
            acc[at, C:] += near[n:n + size, C:]
            n += size

    for k in range(10):
        dr, dc = step_of(k)
        line_at = 0 if dr == 1 else 1
        lr = 0 if dc == 1 else 1

        @pl.when(jnp.logical_not(there(-dr, -dc)))
        def _():
            for stage in range(2):
                for pair in range(2):
                    if k in INNER:
                        ref = halo_i.at[stage, pair, line_at]
                    elif dr == 0:
                        ref = halo_c.at[stage, pair, :, lr]
                    elif dc == 0:
                        ref = halo_o.at[stage, pair, line_at]
                    else:
                        ref = halo_k.at[stage, pair, line_at, lr]
                    ref[...] = jnp.zeros(ref.shape, BF16)

    corners, inners = [], []
    for i in range(2):
        def first(r):
            v = normed_by(tok[i, r].astype(F32), gain1[...])
            put_line(r, 1, silu(v).astype(BF16).astype(F32))
        each(0, ROWS, first, 8)

        def settle(j):
            held[0, i, j] = get_column(j + 1, 0, ROWS).astype(BF16)
        each(0, COLS, settle, 8)
        corners.append(take_lines(0, i, 0, edge_o, corner))
        inners.append(inner_lines())
    corner[0] = jnp.concatenate(corners, axis=0).astype(BF16)
    for line in range(2):
        edge_i[0, line] = jnp.concatenate([inners[0][line], inners[1][line]], axis=0).astype(BF16)

    pl.semaphore_wait(barrier, expected)
    for part in range(2):
        side_sends(0, 0, part, start)
    for part in range(2):
        side_sends(0, 1, part, start)
    for part in range(2):
        tile_sends(0, part, start)

    @pl.when(tm == 0)
    def _():
        for stage in range(2):
            caches[stage].wait()
            corners, inners = [], []
            for i in range(2):
                def turn(r):
                    put_line(r, 1, cache_in[stage, i, r].astype(F32))
                each(0, ROWS, turn, 8)

                def settle(j):
                    halo_t[stage, i, j] = get_column(j + 1, 0, ROWS).astype(BF16)
                each(0, COLS, settle, 8)
                corners.append(take_lines(stage, i, 0, cache_o, cache_k))
                inners.append(inner_lines())
            cache_k[stage] = jnp.concatenate(corners, axis=0).astype(BF16)
            for line in range(2):
                cache_i[stage, line] = jnp.concatenate(
                    [inners[0][line], inners[1][line]], axis=0
                ).astype(BF16)
    for stage in range(2):
        for part in range(2):
            side_sends(stage, 2, part, start)

    for i in range(2):
        def turn(r):
            put_line(r, 1, tok[i, r].astype(F32))
        each(0, ROWS, turn, 8)

        def settle(j):
            tok_t[i, j] = get_column(j + 1, 0, ROWS).astype(BF16)
        each(0, COLS, settle, 8)

    conv_own(0)
    for part in range(2):
        conv_before(0, part)
        corners, inners = [], []
        for i in range(2):
            def second(j):
                v = normed_by(acc[pl.ds(j * ROWS, ROWS), i * C:(i + 1) * C], gain2[...])
                v = silu(v).astype(BF16)
                held[1, i, j] = v
                put_column(j + 1, 0, v.astype(F32))
            for lo, hi in DONE[0][part]:
                each(lo, hi, second, 8)
            if part == 0:
                corners.append(take_lines(1, i, 0, edge_o, corner))
            else:
                inners.append(inner_lines())
        if part == 0:
            corner[1] = jnp.concatenate(corners, axis=0).astype(BF16)
        else:
            for line in range(2):
                edge_i[1, line] = jnp.concatenate([inners[0][line], inners[1][line]], axis=0).astype(BF16)
        side_sends(1, 0, part, start)
        side_sends(1, 1, part, start)
        tile_sends(1, part, start)

    frame = col // 2
    other = 1 - frame
    sent = []

    def send(src, dst, piece, device):
        rel, half, core = dst
        lo, size = PIECES[piece]
        copy = pltpu.make_async_remote_copy(
            src_ref=src.at[pl.ds(lo, size)],
            dst_ref=blocks.at[rel, half, core, pl.ds(lo, size)],
            send_sem=attn_send.at[len(sent)],
            recv_sem=attn_recv.at[rel, half, core, piece],
            device_id=device,
            device_id_type=MESH,
        )
        copy.start()
        sent.append(copy)

    def arrived(rel, half, core, piece):
        lo, size = PIECES[piece]
        ref = blocks.at[rel, half, core, pl.ds(lo, size)]
        pltpu.make_async_remote_copy(
            src_ref=ref, dst_ref=ref,
            send_sem=attn_send.at[0], recv_sem=attn_recv.at[rel, half, core, piece],
            device_id=partner, device_id_type=MESH,
        ).wait_recv()

    conv_own(1)
    for part in range(2):
        conv_before(1, part)
        n = PIECES[part][0]
        for lo, hi in DONE[1][part]:
            for i in range(2):
                def last(j):
                    at = pl.ds(pl.multiple_of(n + (j - lo) * ROWS, ROWS), ROWS)
                    v = acc[pl.ds(pl.multiple_of(j * ROWS, ROWS), ROWS), i * C:(i + 1) * C]
                    v = (v + tok_t[i, j].astype(F32)).astype(BF16)
                    stream[i, at] = v
                    normed[i, at] = normed_by(v.astype(F32), gain_a[...]).astype(BF16)
                each(lo, hi, last, 8)
            n += (hi - lo) * ROWS
        send(normed.at[other], (0, 1, 0), part, partner)
        send(normed.at[frame], (3, 0, 0), part, up)
        send(normed.at[frame], (1, 0, 0), part, down)
        send(normed.at[frame], (0, 0, 1), part, sibling)

    blocks[0, 0, 0] = normed[frame]
    factor = math.log2(math.e) * C ** (-0.5)

    def ask(half):
        q = jnp.dot(blocks[0, half, 0], wq[...], preferred_element_type=F32).astype(BF16)
        q = lax.dot_general(wk[...], q, (((1,), (1,)), ((), ())), preferred_element_type=F32)
        query[:, half * PLACES:(half + 1) * PLACES] = (q * factor).astype(BF16)

    def absorb(rel, half, initial=False):
        keys = blocks[rel, half].reshape(2 * PLACES, C)
        s = jnp.dot(keys, query[...], preferred_element_type=F32)
        now = jnp.max(s, axis=0, keepdims=True)
        if not initial:
            before = top[0:1]
            now = jnp.maximum(before, now)
            shrink = jnp.exp2(before - now)
        expo = jnp.exp2(s - now)
        summed = jnp.sum(expo, axis=0, keepdims=True)
        new = lax.dot_general(
            keys, expo.astype(BF16), (((0,), (0,)), ((), ())), preferred_element_type=F32
        )
        if initial:
            total[0:1] = summed
            mixed[...] = new
        else:
            total[0:1] = total[0:1] * shrink + summed
            mixed[...] = mixed[...] * shrink + new
        top[0:1] = now

    def relay(src, moves):
        for piece in range(2):
            arrived(*src, piece)
            for dst, device in moves:
                send(blocks.at[src], dst, piece, device)

    def ready(rel, half):
        for piece in range(2):
            arrived(rel, half, 1, piece)

    ask(0)
    relay((0, 1, 0), (((3, 1, 0), up), ((1, 1, 0), down), ((0, 1, 1), sibling)))
    ask(1)
    relay((3, 0, 0), (((2, 0, 0), up), ((3, 0, 1), sibling)))
    relay((1, 0, 0), (((1, 0, 1), sibling),))
    ready(0, 0)
    absorb(0, 0, True)
    ready(0, 1)
    absorb(0, 1)
    relay((3, 1, 0), (((3, 1, 1), sibling),))
    relay((1, 1, 0), (((2, 1, 0), down), ((1, 1, 1), sibling)))
    ready(3, 0)
    absorb(3, 0)
    ready(1, 0)
    absorb(1, 0)
    relay((2, 0, 0), (((2, 0, 1), sibling),))
    ready(3, 1)
    absorb(3, 1)
    relay((2, 1, 0), (((2, 1, 1), sibling),))
    ready(1, 1)
    absorb(1, 1)
    ready(2, 0)
    absorb(2, 0)
    ready(2, 1)
    absorb(2, 1)

    def attended(h):
        at = slice(h * PLACES, (h + 1) * PLACES)
        v = (mixed[:, at] / total[0:1, at]).T.astype(BF16)
        return jnp.dot(v, wv[...], preferred_element_type=F32).astype(BF16)

    def finish(i, values):
        acc[:, 0:C] = stream[i].astype(F32) + jnp.dot(values, wo[...], preferred_element_type=F32)
        n = 0
        for part in range(2):
            for lo, hi in DONE[1][part]:
                def put(j):
                    put_column(j + 1, 0, acc[pl.ds(pl.multiple_of(n + (j - lo) * ROWS, ROWS), ROWS), 0:C])
                each(lo, hi, put, 8)
                n += (hi - lo) * ROWS

        def turn(r):
            out[i, r] = get_line(r, 1, COLS).astype(BF16)
        each(0, ROWS, turn, 8)

    mine[...] = attended(1)
    copy = pltpu.make_async_remote_copy(
        src_ref=mine, dst_ref=back, send_sem=back_sem.at[0], recv_sem=back_sem.at[1],
        device_id=partner, device_id_type=MESH,
    )
    copy.start()
    finish(frame, attended(0))
    copy.wait()
    finish(other, back[...])

    for copy in sent:
        copy.wait_send()
    for stage in range(2):
        for part in range(2):
            for group in range(3):
                side_sends(stage, group, part, lambda copy: copy.wait_send())
            tile_sends(stage, part, lambda copy: copy.wait_send())


def on_device(
    tokens, cache_first, cache_second, gain_first, gain_second, conv_first, conv_second,
    gain_attn, query_weight, key_weight, value_weight, out_weight,
):
    vmem = pl.BlockSpec(memory_space=pltpu.VMEM)
    hbm = pl.BlockSpec(memory_space=pl.ANY)
    return pl.pallas_call(
        kernel,
        out_shape=jax.ShapeDtypeStruct(tokens.shape, BF16),
        in_specs=[vmem, hbm, hbm, vmem, vmem, vmem, hbm, hbm, vmem, vmem, vmem, vmem],
        out_specs=vmem,
        scratch_shapes=[
            pltpu.VMEM((2, 3, 3, C, 3 * C), BF16),
            pltpu.VMEM((4, COLS + 2, ROWS, 3 * C), BF16),
            pltpu.VMEM((LANES, COLS + 2, LIFTED, 128), F32),
            pltpu.VMEM((2, COLS, ROWS, C), BF16),
            pltpu.VMEM((2, 2, COLS, ROWS, C), BF16),
            pltpu.VMEM((PLACES, 2 * C), F32),
            pltpu.VMEM((2, 2, ROWS, COLS, C), BF16),
            pltpu.VMEM((2, 2, 2, 16, C), BF16),
            pltpu.VMEM((2, 2, 16, C), BF16),
            pltpu.VMEM((2, 16, C), BF16),
            pltpu.VMEM((2, 2, 2, 16, C), BF16),
            pltpu.VMEM((2, 2, 16, C), BF16),
            pltpu.VMEM((2, 16, C), BF16),
            pltpu.VMEM((2, 2, 2, 2, 16, C), BF16),
            pltpu.VMEM((2, 2, 2, 2, 16, C), BF16),
            pltpu.VMEM((2, 2, 2, 16, C), BF16),
            pltpu.VMEM((2, 2, 2, 2, 16, C), BF16),
            pltpu.VMEM((2, 2, COLS, ROWS, C), BF16),
            pltpu.VMEM((2, PLACES, C), BF16),
            pltpu.VMEM((2, PLACES, C), BF16),
            pltpu.VMEM((4, 2, 2, PLACES, C), BF16),
            pltpu.VMEM((C, 2 * PLACES), BF16),
            pltpu.VMEM((C, 2 * PLACES), F32),
            pltpu.VMEM((8, 2 * PLACES), F32),
            pltpu.VMEM((8, 2 * PLACES), F32),
            pltpu.VMEM((PLACES, C), BF16),
            pltpu.VMEM((PLACES, C), BF16),
            pltpu.SemaphoreType.DMA((2, 3)),
            pltpu.SemaphoreType.DMA((2,)),
            pltpu.SemaphoreType.DMA((2, 3, 14)),
            pltpu.SemaphoreType.DMA((2, 2, 14)),
            pltpu.SemaphoreType.DMA((40,)),
            pltpu.SemaphoreType.DMA((4, 2, 2, 2)),
            pltpu.SemaphoreType.DMA((2,)),
        ],
        compiler_params=pltpu.CompilerParams(
            collective_id=0, has_side_effects=True, vmem_limit_bytes=58 << 20
        ),
    )(
        tokens, cache_first, cache_second, gain_first, gain_second, gain_attn, conv_first, conv_second,
        query_weight, key_weight, value_weight, out_weight,
    )


def solution(mesh):
    spread, kept = P("tm", "row", "col", None), P(None, "row", "col", None)
    return jax.shard_map(
        on_device,
        mesh=mesh,
        in_specs=(spread, kept, kept) + (P(),) * 9,
        out_specs=spread,
        check_vma=False,
    )
```

time: 297 us -> 97.8 us (0.33)
  waiting for transfers between devices: 164 us -> 0 us
  Pallas kernels: 0 us -> 95.7 us
  matrix products: 53.5 us -> 0 us
  starting transfers between devices: 34.5 us -> 0 us
  other arithmetic: 21.1 us -> 0 us
  between operations: 14.1 us -> 0.01 us
  local copies, waits for them, and re-layouts: 9.11 us -> 1.94 us
    all_gather x2 -> x0, waiting for transfers between devices: 131 us -> none  [the longest x1 79.2 us: on_device(): lax.all_gather(keys, ('row', 'col'), axis=1, tiled=True)]
    pallas_call x0 -> x1, Pallas kernels: none -> 95.7 us  [on_device(): pl.pallas_call(kernel, out_shape=jax.ShapeDtypeStruct(tokens.shape, BF16)...]
    dot_general x8 -> x0, matrix products: 53.5 us -> none  [the longest x2 21.1 us: causal_conv(): jnp.dot(stacked, kernel.reshape(27 * chans, chans), preferred_element_typ...]
    ppermute x10 -> x0, starting transfers between devices: 34.2 us -> none  [the longest x4 17.7 us: padded_2(): before = lax.ppermute(last, axis, up)]
    ppermute x10 -> x0, waiting for transfers between devices: 32.5 us -> none  [the longest x2 22.4 us: passed_along(): return lax.ppermute(block, axis, route)]
    reduce_sum x2 -> x0, other arithmetic: 11 us -> none  [the longest x1 9.67 us: absorb(): total = jnp.sum(expo, axis=-1)]
    unnamed x70 -> x1, local copies, waits for them, and re-layouts: 8.56 us -> 1.94 us
    concatenate x6 -> x0, other arithmetic: 5.64 us -> none  [padded_2(): value = jnp.concatenate([before, value, after], axis=dim)]
  transfers between devices with their start and end apart: 12 -> 0, of which waited for: 9 -> 0; matrix products, arithmetic and copies ran while one was open for 10% -> 0% of each run, Pallas kernels for 0% -> 0%
where the time goes in v2:
time: 97.8 us; the launch traced here: 97.6 us
  Pallas kernels  95.7 us (98%)
  local copies, waits for them, and re-layouts  1.94 us (2%)
    pallas_call x1, Pallas kernels, on_device(): pl.pallas_call(kernel, out_shape=jax.ShapeDtypeStruct(tokens.shape, BF16)...  95.7 us

profile of v2, /device:TPU:1, one launch (start us, length us, event | category | flops | bytes accessed | tf_op | source)
XLA Modules:
  0.0 97.6 jit_solution(11589435481989340297)
XLA Ops:
  0.0 95.7 %shard_map.118 = bf16[2,16,24,384]{3,2,1,0:T(8,128)(2,1)} custom-call(bf16[2,16,24,384]{3,2,1,0:T(8,128)(2,1)} %tok.1, bf16[2,16,24,384]{3,2,1,0:T(8,128)(2,1)} %cache1.1, bf16[2,16,24,384]{3,2,1,0:T(8,128)(2,1)} %cache2.1, f32[384]{0:T(512)} %gain1.1, f32[384]{0:T(512)} %gain2.1, f32[384]{0:T(512)} %gain_a.1, bf16[3,3,3,384,384]{4,3,2,1,0:T(8,128)(2,1)} %w1.1, ...), custom_call_target="tpu_custom_call" | custom-call | tf_op jit(solution)/shard_map/pallas_call | solution.py:559
  95.7 1.9 %copy.14 = bf16[2,16,24,384]{3,2,1,0:T(8,128)(2,1)} copy(bf16[2,16,24,384]{3,2,1,0:T(8,128)(2,1)} %shard_map.118) | data formatting | bytes 1179648
